TPU v7x, 32 devices: a whole 2x2x4 slice. The times are simulated.
32 devices in a mesh: region: 16 (over z, y, x), blk: 2 (over core).
Axes of the slice: x: 2, y: 2, z: 4, core: 2. Of those that a mesh axis runs over, the one named last changes fastest.
Arguments:
- site_tensors: float32 [128, 2, 32, 1024], P('region', 'blk'), may hold values from -18 to 18
- projectors: bfloat16 [128, 2, 32, 1024], P('region'), may hold values from -0.1875 to 0.1875
- gate_matrix: float32 [2, 2, 2, 2], replicated, may hold values from -3 to 3
- recv_src: int32 [128, 3], P('region'), may hold values from 0 to 88, as said below
- cut_list: int32 [160], P('region'), may hold values from 0 to 23, as said below
- cut_dest: int32 [16, 10], replicated, may hold values from -1 to 63, as said below
- gate_src: int32 [128], P('region'), may hold values from 0 to 24, as said below
- gate_list: int32 [32], P('region'), may hold values from 0 to 7, as said below
- gate_dest: int32 [16, 2], replicated, may hold values from -1 to 15, as said below
Outputs:
- new_sites: float32 [128, 2, 32, 1024], P('region', 'blk')
- messages: float32 [128, 3, 1024], P('region')
Inputs may be any that keep to these rules, and one draw needn't show every extreme that they name: `recv_src`: messages between one ordered pair of regions use distinct slots below 4; some pair uses all 4. `cut_list`: entries whose cut_dest is -1 are padding. `cut_dest`: some region fills all 10 entries of its row. `gate_src`: gate partners form pairs along vertical links. `gate_list`: entries whose gate_dest is -1 are padding. `gate_dest`: some region fills all 2 entries of its row.
All inputs are finite; a program needn't handle non-finite values.
Results may differ from a plain program's by a relative error of at most 0.0039.
Values may be sent and summed in bfloat16 or wider, within the bound.
A program may use at most 128 MiB of HBM per device.

v0:
```python
import jax
import jax.numpy as jnp
from jax import lax
from jax.sharding import PartitionSpec as P

SWEEPS = 2
CAP = 4
GCAP = 1
HIGHEST = lax.Precision.HIGHEST
EPSILON = 1e-06


def weighted(tensors, incoming):
    partial_a = jnp.einsum("isabc,iag->isgbc", tensors, incoming[:, 0], precision=HIGHEST)
    return jnp.einsum("isgbc,ibe->isgec", partial_a, incoming[:, 1], precision=HIGHEST)


def outgoing(tensors, incoming):
    partial_c = jnp.einsum("isabc,icd->isabd", tensors, incoming[:, 2], precision=HIGHEST)
    both_bc = jnp.einsum("isabd,ibe->isaed", partial_c, incoming[:, 1], precision=HIGHEST)
    leg_zero = jnp.einsum("isaed,isfed->iaf", both_bc, tensors, precision=HIGHEST)
    both_ac = jnp.einsum("isabd,iag->isgbd", partial_c, incoming[:, 0], precision=HIGHEST)
    leg_one = jnp.einsum("isgbd,isghd->ibh", both_ac, tensors, precision=HIGHEST)
    both_ab = weighted(tensors, incoming)
    leg_two = jnp.einsum("isgec,isgek->ick", both_ab, tensors, precision=HIGHEST)
    return jnp.stack([leg_zero, leg_one, leg_two], axis=1)


def normalized(leg_terms):
    trace_sum = jnp.trace(leg_terms, axis1=2, axis2=3)
    return leg_terms.shape[-1] * leg_terms / trace_sum[:, :, None, None]


def select_rows(dest_table, my_region, capacity):
    region_count, columns = dest_table.shape
    wanted = my_region * capacity + jnp.arange(capacity, dtype=jnp.int32)
    matched = dest_table[:, :, None] == wanted[None, None, :]
    position = jnp.sum(
        jnp.where(matched, jnp.arange(columns, dtype=jnp.int32)[None, :, None], 0), axis=1
    )
    return (jnp.arange(region_count, dtype=jnp.int32)[:, None] * columns + position).reshape(-1)


def shards(
    site_tensors,
    projectors,
    gate_matrix,
    recv_src,
    cut_list,
    cut_dest,
    gate_src,
    gate_list,
    gate_dest,
):
    site_count = site_tensors.shape[0]
    bond_dim = site_tensors.shape[2]
    regions = lax.axis_size("region")
    my_region = lax.axis_index("region")
    my_spin = lax.axis_index("blk")
    tensors = site_tensors.reshape(site_count, 1, bond_dim, bond_dim, bond_dim)
    boundary = jnp.zeros((bond_dim, bond_dim), jnp.float32).at[0, 0].set(bond_dim)
    identity = jnp.eye(bond_dim, dtype=jnp.float32)
    msg_none = 3 * site_count + regions * CAP
    incoming = jnp.where((recv_src == msg_none)[:, :, None, None], boundary, identity)
    edge_row = boundary.reshape(1, bond_dim * bond_dim)
    for sweep_index in range(SWEEPS):
        totals = lax.psum(outgoing(tensors, incoming), "blk")
        fresh_msgs = normalized(totals).reshape(3 * site_count, bond_dim * bond_dim)
        leaving = fresh_msgs[cut_list]
        everyone = lax.all_gather(leaving, "region", axis=0, tiled=True)
        arrived = everyone[select_rows(cut_dest, my_region, CAP)]
        lookup = jnp.concatenate([fresh_msgs, arrived, edge_row], axis=0)
        incoming = lookup[recv_src].reshape(site_count, 3, bond_dim, bond_dim)
    messages = incoming.reshape(site_count, 3, bond_dim * bond_dim)
    weights = (
        weighted(tensors, incoming)
        .astype(jnp.bfloat16)
        .reshape(site_count, bond_dim * bond_dim, bond_dim)
    )
    factor = jnp.einsum(
        "ikc,isnk->icsn", weights, projectors, preferred_element_type=jnp.float32
    ).astype(jnp.bfloat16)
    factor = factor.reshape(site_count, 1, bond_dim, 2 * bond_dim)
    halves = lax.all_gather(factor, "blk", axis=1, tiled=True)
    flat_factor = halves.reshape(site_count, 4 * bond_dim * bond_dim)
    leaving_factor = flat_factor[gate_list]
    everyone_factor = lax.all_gather(leaving_factor, "region", axis=0, tiled=True)
    arrived_factor = everyone_factor[select_rows(gate_dest, my_region, GCAP)]
    empty_row = jnp.zeros((1, 4 * bond_dim * bond_dim), jnp.bfloat16)
    factor_lookup = jnp.concatenate([flat_factor, arrived_factor, empty_row], axis=0)
    partners = factor_lookup[gate_src].reshape(site_count, 2, bond_dim, 2, bond_dim)
    mixing = jnp.einsum(
        "ajby,iycjn->iabcn", gate_matrix, partners.astype(jnp.float32), precision=HIGHEST
    )
    own_old = lax.dynamic_index_in_dim(mixing, my_spin, 2, keepdims=False)
    spin_piece = jnp.einsum("iuvc,iacn->iauvn", tensors[:, 0], own_old, precision=HIGHEST)
    spin_piece = spin_piece.reshape(site_count, 2, bond_dim, bond_dim * bond_dim)
    summed = lax.psum_scatter(spin_piece, "blk", scatter_dimension=1, tiled=True)
    squares = jnp.sum(summed * summed, axis=(1, 2, 3))
    total_sq = lax.psum(squares, "blk")
    mean_sq = total_sq / (2 * bond_dim**3)
    updated = summed / jnp.sqrt(mean_sq + EPSILON)[:, None, None, None]
    unchanged = gate_src == site_count + regions * GCAP
    new_sites = jnp.where(unchanged[:, None, None, None], site_tensors, updated)
    return (new_sites, messages)


def solution(mesh):
    return jax.shard_map(
        shards,
        mesh=mesh,
        in_specs=(
            P("region", "blk", None, None),
            P("region", None, None, None),
            P(),
            P("region", None),
            P("region"),
            P(),
            P("region"),
            P("region"),
            P(),
        ),
        out_specs=(P("region", "blk", None, None), P("region", None, None)),
        check_vma=False,
    )
```

profile of v0, /device:TPU:0, one launch (start us, length us, event | category | flops | bytes accessed | tf_op | source)
XLA Modules:
  0.0 483.6 jit_solution(1316465474755128273)
XLA Ops:
  7.2 0.8 broadcast_compare_fusion
  8.0 3.9 reshape.220
  11.9 6.4 %copy.94 = f32[8,32,32,32]{2,1,3,0:T(8,128)} copy(f32[8,32,32,32]{3,2,1,0:T(8,128)} %reshape.220) | data formatting | bytes 2097152 | tf_op jit(solution)/shard_map/reshape.47
  18.4 20.8 %convolution_bitcast_fusion.3 = f32[8,32,32,32]{2,3,1,0:T(8,128)S(1)} fusion(f32[8,32,32,32]{3,2,1,0:T(8,128)} %reshape.220, f32[8,3,32,32]{2,3,0,1:T(8,128)S(1)} %broadcast_select_fusion), kind=kOutput, calls=%fused_computation.35 | convolution fusion | flops 100663296 | bytes 2228224 | tf_op jit(solution)/shard_map/isabc,icd->isabd/dot_general | solution.py:19
  39.2 9.3 %fusion.14 = f32[8,32,32,32]{1,2,3,0:T(8,128)} fusion(f32[8,32,32,32]{2,3,1,0:T(8,128)S(1)} %convolution_bitcast_fusion.3, f32[8,3,32,32]{2,3,0,1:T(8,128)S(1)} %broadcast_select_fusion), kind=kOutput, calls=%fused_computation.23 | convolution fusion | flops 100663296 | bytes 5373952 | tf_op jit(solution)/shard_map/isabd,iag->isgbd/dot_general | solution.py:22
  48.5 20.6 %convolution_bitcast_fusion.2 = f32[8,32,32,32]{3,2,1,0:T(8,128)} fusion(f32[8,32,32,32]{2,3,1,0:T(8,128)S(1)} %convolution_bitcast_fusion.3, f32[8,3,32,32]{2,3,0,1:T(8,128)S(1)} %broadcast_select_fusion), kind=kOutput, calls=%fused_computation.34 | convolution fusion | flops 100663296 | bytes 5373952 | tf_op jit(solution)/shard_map/isabd,ibe->isaed/dot_general | solution.py:20
  69.1 6.8 %fusion.20 = f32[8,32,32,32]{3,1,2,0:T(8,128)} fusion(f32[8,32,32,32]{3,2,1,0:T(8,128)S(1)} %copy-done.1, f32[8,3,32,32]{2,3,0,1:T(8,128)S(1)} %broadcast_select_fusion), kind=kOutput, calls=%fused_computation.29 | convolution fusion | flops 100663296 | bytes 5373952 | tf_op jit(solution)/shard_map/isabc,iag->isgbc/dot_general | solution.py:14
  75.9 6.6 %copy.93 = f32[8,32,32,32]{2,1,3,0:T(8,128)} copy(f32[8,32,32,32]{3,2,1,0:T(8,128)} %convolution_bitcast_fusion.2) | data formatting | bytes 2097152 | tf_op jit(solution)/shard_map/reshape.51
  82.5 9.7 %convolution_bitcast_fusion.7 = f32[8,1,32,32]{3,2,0,1:T(8,128)S(1)} fusion(f32[8,32,32,32]{1,2,3,0:T(8,128)} %fusion.14, f32[8,32,32,32]{2,1,3,0:T(8,128)} %copy.94), kind=kOutput, calls=%fused_computation.43 | convolution fusion | flops 100663296 | bytes 2129920 | tf_op jit(solution)/shard_map/isgbd,isghd->ibh/dot_general | solution.py:23
  92.3 4.1 convolution_bitcast_fusion.8
  96.5 6.6 %fusion.12 = f32[8,32,32,32]{3,1,2,0:T(8,128)S(1)} fusion(f32[8,32,32,32]{3,1,2,0:T(8,128)S(1)} %copy-done.8, f32[8,3,32,32]{2,3,0,1:T(8,128)S(1)} %broadcast_select_fusion), kind=kOutput, calls=%fused_computation.21 | convolution fusion | flops 100663296 | bytes 5373952 | tf_op jit(solution)/shard_map/isgbc,ibe->isgec/dot_general | solution.py:15
  103.1 7.0 %fusion.28 = f32[8,1,32,32]{3,2,0,1:T(8,128)S(1)} fusion(f32[8,32,32,32]{3,2,1,0:T(8,128)S(1)} %copy-done.2, f32[8,32,32,32]{3,1,2,0:T(8,128)S(1)} %fusion.12), kind=kOutput, calls=%fused_computation.39 | convolution fusion | flops 100663296 | bytes 2129920 | tf_op jit(solution)/shard_map/isgec,isgek->ick/dot_general | solution.py:25
  110.2 0.8 pad_maximum_fusion.2
  111.1 2.7 reshape.344
  114.8 17.5 %all-reduce.5.cloned.1.call-done = f32[8,3,32,32]{3,2,0,1:T(8,128)} async-done(((f32[8,3,32,32]{3,2,0,1:T(8,128)}), f32[8,3,32,32]{3,2,0,1:T(8,128)}) %all-reduce.5.cloned.1.call-update) | async-done | bytes 98320 | tf_op jit(solution)/shard_map/psum | solution.py:67
  132.3 1.2 select_reduce_fusion.1
  133.4 1.1 multiply_divide_fusion.1
  135.3 49.6 %all-gather.3 = f32[16,10,1024]{2,1,0:T(8,128)} all-gather(f32[1,10,1024]{2,1,0:T(8,128)S(1)} %bitcast.197), channel_id=2, replica_groups=mesh['region'=16,'blk'=2] {'region'}, dimensions={0}, use_global_device_ids=true | all-gather | bytes 696320 | tf_op jit(solution)/shard_map/all_gather | solution.py:70
  185.0 1.3 reshape.320
  187.8 21.2 %convolution_bitcast_fusion.1 = f32[8,32,32,32]{2,3,1,0:T(8,128)S(1)} fusion(f32[8,32,32,32]{3,2,1,0:T(8,128)} %reshape.220, f32[8,3,32,32]{3,2,1,0:T(8,128)S(1)} %reshape.224), kind=kOutput, calls=%fused_computation.33 | convolution fusion | flops 100663296 | bytes 2228224 | tf_op jit(solution)/shard_map/isabc,icd->isabd/dot_general | solution.py:19
  209.0 8.4 %fusion.10 = f32[8,32,32,32]{1,2,3,0:T(8,128)S(1)} fusion(f32[8,32,32,32]{2,3,1,0:T(8,128)S(1)} %convolution_bitcast_fusion.1, f32[8,3,32,32]{3,2,1,0:T(8,128)S(1)} %reshape.224), kind=kOutput, calls=%fused_computation.19 | convolution fusion | flops 100663296 | bytes 5373952 | tf_op jit(solution)/shard_map/isabd,iag->isgbd/dot_general | solution.py:22
  217.4 21.1 %convolution_bitcast_fusion = f32[8,32,32,32]{3,2,1,0:T(8,128)} fusion(f32[8,32,32,32]{2,3,1,0:T(8,128)S(1)} %convolution_bitcast_fusion.1, f32[8,3,32,32]{3,2,1,0:T(8,128)S(1)} %reshape.224), kind=kOutput, calls=%fused_computation.32 | convolution fusion | flops 100663296 | bytes 5373952 | tf_op jit(solution)/shard_map/isabd,ibe->isaed/dot_general | solution.py:20
  238.5 6.9 %fusion.18 = f32[8,32,32,32]{3,1,2,0:T(8,128)} fusion(f32[8,32,32,32]{3,2,1,0:T(8,128)S(1)} %copy-done.3, f32[8,3,32,32]{3,2,1,0:T(8,128)S(1)} %reshape.224), kind=kOutput, calls=%fused_computation.27 | convolution fusion | flops 100663296 | bytes 5373952 | tf_op jit(solution)/shard_map/isabc,iag->isgbc/dot_general | solution.py:14
  245.4 6.3 %convolution_bitcast_fusion.5 = f32[8,1,32,32]{3,2,0,1:T(8,128)S(1)} fusion(f32[8,32,32,32]{1,2,3,0:T(8,128)S(1)} %fusion.10, f32[8,32,32,32]{2,1,3,0:T(8,128)S(1)} %copy-done.6), kind=kOutput, calls=%fused_computation.41 | convolution fusion | flops 100663296 | bytes 2129920 | tf_op jit(solution)/shard_map/isgbd,isghd->ibh/dot_general | solution.py:23
  251.7 6.5 %copy.109 = f32[8,32,32,32]{2,1,3,0:T(8,128)} copy(f32[8,32,32,32]{3,2,1,0:T(8,128)} %convolution_bitcast_fusion) | data formatting | bytes 2097152 | tf_op jit(solution)/shard_map/reshape.70
  258.2 7.7 %convolution_bitcast_fusion.6 = f32[8,1,32,32]{3,2,0,1:T(8,128)S(1)} fusion(f32[8,32,32,32]{2,1,3,0:T(8,128)} %copy.109, f32[8,32,32,32]{2,1,3,0:T(8,128)} %copy.94), kind=kOutput, calls=%fused_computation.42 | convolution fusion | flops 100663296 | bytes 2129920 | tf_op jit(solution)/shard_map/isaed,isfed->iaf/dot_general | solution.py:21
  266.0 6.2 %fusion.8 = f32[8,32,32,32]{3,1,2,0:T(8,128)S(1)} fusion(f32[8,32,32,32]{3,1,2,0:T(8,128)S(1)} %copy-done.7, f32[8,3,32,32]{3,2,1,0:T(8,128)S(1)} %reshape.224), kind=kOutput, calls=%fused_computation.17 | convolution fusion | flops 100663296 | bytes 5373952 | tf_op jit(solution)/shard_map/isgbc,ibe->isgec/dot_general | solution.py:15
  272.2 7.2 %fusion.31 = f32[8,1,32,32]{3,2,0,1:T(8,128)S(1)} fusion(f32[8,32,32,32]{3,2,1,0:T(8,128)S(1)} %copy-done.4, f32[8,32,32,32]{3,1,2,0:T(8,128)S(1)} %fusion.8), kind=kOutput, calls=%fused_computation.40 | convolution fusion | flops 100663296 | bytes 2129920 | tf_op jit(solution)/shard_map/isgec,isgek->ick/dot_general | solution.py:25
  279.4 0.8 pad_maximum_fusion.3
  280.2 14.5 %all-reduce.7.cloned.1.call-done = f32[8,3,32,32]{3,2,0,1:T(8,128)} async-done(((f32[8,3,32,32]{3,2,0,1:T(8,128)}), f32[8,3,32,32]{3,2,0,1:T(8,128)}) %all-reduce.7.cloned.1.call-update) | async-done | bytes 98320 | tf_op jit(solution)/shard_map/psum | solution.py:67
  294.7 1.2 select_reduce_fusion
  295.9 1.1 multiply_divide_fusion
  297.7 49.6 %all-gather.4 = f32[16,10,1024]{2,1,0:T(8,128)} all-gather(f32[1,10,1024]{2,1,0:T(8,128)S(1)} %bitcast.196), channel_id=3, replica_groups=mesh['region'=16,'blk'=2] {'region'}, dimensions={0}, use_global_device_ids=true | all-gather | bytes 696320 | tf_op jit(solution)/shard_map/all_gather | solution.py:70
  347.4 1.3 reshape.322
  350.1 8.3 %fusion.16 = f32[8,32,32,32]{3,1,2,0:T(8,128)S(1)} fusion(f32[8,32,32,32]{3,2,1,0:T(8,128)} %reshape.220, f32[8,3,32,32]{3,2,1,0:T(8,128)S(1)} %reshape.228), kind=kOutput, calls=%fused_computation.25 | convolution fusion | flops 100663296 | bytes 2228224 | tf_op jit(solution)/shard_map/isabc,iag->isgbc/dot_general | solution.py:14
  358.5 5.6 %fusion.25 = bf16[8,32,32,32]{3,1,2,0:T(8,128)(2,1)S(1)} fusion(f32[8,32,32,32]{3,1,2,0:T(8,128)S(1)} %fusion.16, f32[8,3,32,32]{3,2,1,0:T(8,128)S(1)} %reshape.228), kind=kOutput, calls=%fused_computation.36 | convolution fusion | flops 100925440 | bytes 4849664 | tf_op jit(solution)/shard_map/isgbc,ibe->isgec/dot_general | solution.py:15
  364.1 0.9 convolution_convert_fusion
  365.3 2.2 all_gather.14
  368.2 37.0 %all-gather.5 = bf16[16,2,4096]{2,1,0:T(2,128)(2,1)S(1)} all-gather(bf16[1,2,4096]{2,1,0:T(2,128)(2,1)S(1)} %bitcast.198), channel_id=4, replica_groups=mesh['region'=16,'blk'=2] {'region'}, dimensions={0}, use_global_device_ids=true | all-gather | bytes 278528 | tf_op jit(solution)/shard_map/all_gather | solution.py:87
  406.8 1.1 convolution_bitcast_fusion.4
  408.2 24.5 %fusion.22 = f32[8,2,32,32,32]{3,4,2,1,0:T(8,128)} fusion(f32[8,32,32,32,1]{3,2,1,0,4:T(8,128)} %reshape.344, f32[8,2,32,32,1]{3,1,2,0,4:T(2,128)S(1)} %bitcast.195), kind=kOutput, calls=%fused_computation.31 | convolution fusion | flops 201326592 | bytes 3211264 | tf_op jit(solution)/shard_map/iuvc,iacn->iauvn/dot_general | solution.py:96
  432.7 9.0 %copy.129 = f32[8,2,32,32,32]{4,3,2,1,0:T(8,128)} copy(f32[8,2,32,32,32]{3,4,2,1,0:T(8,128)} %fusion.22) | data formatting | bytes 4194304 | tf_op jit(solution)/shard_map/iuvc,iacn->iauvn/transpose | solution.py:96
  441.6 7.7 %reshape.233 = f32[8,2,32,1024]{3,2,1,0:T(8,128)} reshape(f32[8,2,32,32,32]{4,3,2,1,0:T(8,128)} %copy.129) | data formatting | bytes 4194304 | tf_op jit(solution)/shard_map/reshape | solution.py:97
  450.0 18.5 %all-reduce.9.cloned.1.call-done = f32[8,2,32,1024]{3,2,1,0:T(8,128)} async-done(((f32[8,2,32,1024]{3,2,1,0:T(8,128)}), f32[8,2,32,1024]{3,2,1,0:T(8,128)}) %all-reduce.9.cloned.1.call-update) | async-done | bytes 2097168
  468.5 2.0 multiply_reduce_fusion
  470.5 0.7 copy.130
  471.2 2.4 psum.23
  473.6 3.0 divide_select_fusion
  (105 shorter events, 9.2 us)
Async XLA Ops:
  7.2 356.9 %copy-start = (bf16[8,2,32,1024]{3,2,1,0:T(8,128)(2,1)S(1)}, bf16[8,2,32,1024]{3,2,1,0:T(8,128)(2,1)}, u32[]{:S(2)}) copy-start(bf16[8,2,32,1024]{3,2,1,0:T(8,128)(2,1)} %param.12) | copy-start | bytes 3145732
  7.2 125.1 %all-reduce.5.cloned.1.call-start = ((), (), s32[]{:S(2)}) async-start(), calls=%async_computation | async-start | bytes 786432 | tf_op jit(solution)/shard_map/psum | solution.py:67
  11.9 6.4 %copy-start.12 = (f32[32,32]{0,1:T(8,128)S(1)}, f32[32,32]{0,1:T(8,128)}, u32[]{:S(2)}) copy-start(f32[32,32]{0,1:T(8,128)} %constant.75.clone.1) | copy-start | bytes 12292
  48.5 20.6 %copy-start.1 = (f32[8,32,32,32]{3,2,1,0:T(8,128)S(1)}, f32[8,32,32,32]{3,2,1,0:T(8,128)}, u32[]{:S(2)}) copy-start(f32[8,32,32,32]{3,2,1,0:T(8,128)} %reshape.220) | copy-start | bytes 3145732
  82.5 9.8 %copy-start.5 = (f32[8,32,32,32]{2,1,3,0:T(8,128)S(1)}, f32[8,32,32,32]{2,1,3,0:T(8,128)}, u32[]{:S(2)}) copy-start(f32[8,32,32,32]{2,1,3,0:T(8,128)} %copy.94) | copy-start | bytes 3145732
  82.5 9.8 %copy-start.9 = (f32[8,32,32,32]{2,1,3,0:T(8,128)S(1)}, f32[8,32,32,32]{2,1,3,0:T(8,128)}, u32[]{:S(2)}) copy-start(f32[8,32,32,32]{2,1,3,0:T(8,128)} %copy.93) | copy-start | bytes 3145732
  92.3 4.1 copy-start.8
  96.4 6.6 %copy-start.2 = (f32[8,32,32,32]{3,2,1,0:T(8,128)S(1)}, f32[8,32,32,32]{3,2,1,0:T(8,128)}, u32[]{:S(2)}) copy-start(f32[8,32,32,32]{3,2,1,0:T(8,128)} %reshape.220) | copy-start | bytes 3145732
  103.1 7.9 %copy-start.13 = (s32[8,3]{0,1:T(4,128)S(1)}, s32[8,3]{0,1:T(4,128)}, u32[]{:S(2)}) copy-start(s32[8,3]{0,1:T(4,128)} %param.14) | copy-start | bytes 292
  103.1 8.0 %copy-start.10 = (f32[8,1,32,1024]{3,2,1,0:T(8,128)S(1)}, f32[8,1,32,1024]{3,2,1,0:T(8,128)}, u32[]{:S(2)}) copy-start(f32[8,1,32,1024]{3,2,1,0:T(8,128)} %param.11) | copy-start | bytes 3145732
  110.1 3.7 copy-start.16
  110.1 3.7 copy-start.17
  110.1 3.8 copy-start.18
  110.1 3.8 copy-start.19
  110.1 4.0 copy-start.15
  110.1 4.2 copy-start.14
  111.0 183.7 %all-reduce.7.cloned.1.call-start = ((), (), s32[]{:S(2)}) async-start(), calls=%async_computation.1 | async-start | bytes 786432 | tf_op jit(solution)/shard_map/psum | solution.py:67
  113.8 73.2 %copy-start.11 = (f32[1,1024]{1,0:T(1,128)S(1)}, f32[1,1024]{1,0:T(1,128)}, u32[]{:S(2)}) copy-start(f32[1,1024]{1,0:T(1,128)} %constant.84.clone.1) | copy-start | bytes 12292
  217.4 21.2 %copy-start.3 = (f32[8,32,32,32]{3,2,1,0:T(8,128)S(1)}, f32[8,32,32,32]{3,2,1,0:T(8,128)}, u32[]{:S(2)}) copy-start(f32[8,32,32,32]{3,2,1,0:T(8,128)} %reshape.220) | copy-start | bytes 3145732
  238.5 6.9 %copy-start.6 = (f32[8,32,32,32]{2,1,3,0:T(8,128)S(1)}, f32[8,32,32,32]{2,1,3,0:T(8,128)}, u32[]{:S(2)}) copy-start(f32[8,32,32,32]{2,1,3,0:T(8,128)} %copy.94) | copy-start | bytes 3145732
  258.2 7.7 %copy-start.7 = (f32[8,32,32,32]{3,1,2,0:T(8,128)S(1)}, f32[8,32,32,32]{3,1,2,0:T(8,128)}, u32[]{:S(2)}) copy-start(f32[8,32,32,32]{3,1,2,0:T(8,128)} %fusion.18) | copy-start | bytes 3145732
  266.0 6.2 %copy-start.4 = (f32[8,32,32,32]{3,2,1,0:T(8,128)S(1)}, f32[8,32,32,32]{3,2,1,0:T(8,128)}, u32[]{:S(2)}) copy-start(f32[8,32,32,32]{3,2,1,0:T(8,128)} %reshape.220) | copy-start | bytes 3145732
  280.2 188.3 %all-reduce.9.cloned.1.call-start = ((), (), s32[]{:S(2)}) async-start(), calls=%async_computation.2 | async-start | bytes 4194304
  441.6 7.7 %copy-start.20 = (u32[32]{0:T(128)S(1)}, u32[32]{0:T(128)}, u32[]{:S(2)}) copy-start(u32[32]{0:T(128)} %constant.101) | copy-start | bytes 388
Sparse Core Ops, SparseCore 0:
  111.1 21.1 all-reduce.4
  280.3 14.3 all-reduce.6
  449.5 19.0 all-reduce.8
where the time goes:
time: 492 us; the launch traced here: 484 us
  matrix products  210 us (43%)
  blocking collectives  141 us (29%)
  local copies, waits for them, and re-layouts  54.7 us (11%)
  waiting for transfers between devices  50.5 us (10%)
  between operations  14.8 us (3%)
  other arithmetic  12.3 us (2%)
    all_gather x2, blocking collectives, shards(): everyone = lax.all_gather(leaving, 'region', axis=0, tiled=True)  99.2 us
    dot_general x2, matrix products, outgoing(): jnp.einsum('isabc,icd->isabd', tensors, incoming[:, 2], precision=HIGHEST)  42 us
    dot_general x2, matrix products, outgoing(): jnp.einsum('isabd,ibe->isaed', partial_c, incoming[:, 1], precision=HIGHEST)  41.8 us
    all_gather x1, blocking collectives, shards(): lax.all_gather(leaving_factor, 'region', axis=0, tiled=True)  37 us
    psum x2, waiting for transfers between devices, shards(): totals = lax.psum(outgoing(tensors, incoming), 'blk')  32 us
    another operation x6, local copies, waits for them, and re-layouts  26.4 us
    dot_general x1, matrix products, shards(): jnp.einsum('iuvc,iacn->iauvn', tensors[:, 0], own_old, precision=HIGHEST)  24.5 us
    dot_general x3, matrix products, weighted(): jnp.einsum('isabc,iag->isgbc', tensors, incoming[:, 0], precision=HIGHEST)  22.1 us
  transfers between devices with their start and end apart: 3, of which 3 were waited for; matrix products, arithmetic and copies ran while one was open for 1% of the time, Pallas kernels for 0%

commit v1 on v0

--- a/solution.py
+++ b/solution.py
@@ -8,6 +8,24 @@
 GCAP = 1
 HIGHEST = lax.Precision.HIGHEST
 EPSILON = 1e-06
+
+
+def gather_around(shard, axis, dim):
+    ways, here, lap = (lax.axis_size(axis), lax.axis_index(axis), shard.shape[dim])
+    shape = [n * ways if d == dim else n for d, n in enumerate(shard.shape)]
+    full = lax.dynamic_update_slice_in_dim(
+        jnp.zeros(shape, shard.dtype), shard, here * lap, axis=dim
+    )
+    going_up = going_down = shard
+    for far in range(1, ways // 2 + 1):
+        going_up = lax.ppermute(going_up, axis, [(d, (d + 1) % ways) for d in range(ways)])
+        full = lax.dynamic_update_slice_in_dim(full, going_up, (here - far) % ways * lap, axis=dim)
+        if 2 * far < ways:
+            going_down = lax.ppermute(going_down, axis, [(d, (d - 1) % ways) for d in range(ways)])
+            full = lax.dynamic_update_slice_in_dim(
+                full, going_down, (here + far) % ways * lap, axis=dim
+            )
+    return full
 
 
 def weighted(tensors, incoming):
@@ -84,7 +102,7 @@
     halves = lax.all_gather(factor, "blk", axis=1, tiled=True)
     flat_factor = halves.reshape(site_count, 4 * bond_dim * bond_dim)
     leaving_factor = flat_factor[gate_list]
-    everyone_factor = lax.all_gather(leaving_factor, "region", axis=0, tiled=True)
+    everyone_factor = gather_around(leaving_factor, "region", 0)
     arrived_factor = everyone_factor[select_rows(gate_dest, my_region, GCAP)]
     empty_row = jnp.zeros((1, 4 * bond_dim * bond_dim), jnp.bfloat16)
     factor_lookup = jnp.concatenate([flat_factor, arrived_factor, empty_row], axis=0)

time: 492 us -> 512 us (1.041)
  starting transfers between devices: 0.12 us -> 39.7 us
  blocking collectives: 141 us -> 104 us
  waiting for transfers between devices: 50.5 us -> 67 us
    ppermute x0 -> x15, starting transfers between devices: none -> 39.6 us  [the longest x7 39.3 us: gather_around(): lax.ppermute(going_down, axis, [(d, (d - 1) % ways) for d in range(ways)])]
    all_gather x1 -> x0, blocking collectives: 37 us -> none  [shards(): lax.all_gather(leaving_factor, 'region', axis=0, tiled=True)]
    ppermute x0 -> x15, waiting for transfers between devices: none -> 18.8 us  [the longest x8 18.8 us: gather_around(): lax.ppermute(going_up, axis, [(d, (d + 1) % ways) for d in range(ways)])]
  transfers between devices with their start and end apart: 3 -> 18, of which waited for: 3 -> 11; matrix products, arithmetic and copies ran while one was open for 1% -> 1% of each run, Pallas kernels for 0% -> 0%
where the time goes in v1:
time: 512 us; the launch traced here: 503 us
  matrix products  210 us (41%)
  blocking collectives  104 us (20%)
  waiting for transfers between devices  67 us (13%)
  local copies, waits for them, and re-layouts  55.7 us (11%)
  starting transfers between devices  39.7 us (8%)
  between operations  15.2 us (3%)
  other arithmetic  12.4 us (2%)
    all_gather x2, blocking collectives, shards(): everyone = lax.all_gather(leaving, 'region', axis=0, tiled=True)  99.2 us
    dot_general x2, matrix products, outgoing(): jnp.einsum('isabc,icd->isabd', tensors, incoming[:, 2], precision=HIGHEST)  42.2 us
    dot_general x2, matrix products, outgoing(): jnp.einsum('isabd,ibe->isaed', partial_c, incoming[:, 1], precision=HIGHEST)  41.6 us
    ppermute x7, starting transfers between devices, gather_around(): lax.ppermute(going_down, axis, [(d, (d - 1) % ways) for d in range(ways)])  39.3 us
    psum x2, waiting for transfers between devices, shards(): totals = lax.psum(outgoing(tensors, incoming), 'blk')  31.6 us
    another operation x6, local copies, waits for them, and re-layouts  27 us
    dot_general x1, matrix products, shards(): jnp.einsum('iuvc,iacn->iauvn', tensors[:, 0], own_old, precision=HIGHEST)  24.5 us
    dot_general x3, matrix products, weighted(): jnp.einsum('isabc,iag->isgbc', tensors, incoming[:, 0], precision=HIGHEST)  22.1 us
  transfers between devices with their start and end apart: 18, of which 11 were waited for; matrix products, arithmetic and copies ran while one was open for 1% of the time, Pallas kernels for 0%

profile of v1, /device:TPU:0, one launch (start us, length us, event | category | flops | bytes accessed | tf_op | source)
XLA Modules:
  0.0 503.5 jit_solution(2931855762606209351)
XLA Ops:
  8.0 3.9 reshape.220
  11.9 6.4 %copy.94 = f32[8,32,32,32]{2,1,3,0:T(8,128)} copy(f32[8,32,32,32]{3,2,1,0:T(8,128)} %reshape.220) | data formatting | bytes 2097152 | tf_op jit(solution)/shard_map/reshape.47
  18.5 20.8 %convolution_bitcast_fusion.3 = f32[8,32,32,32]{2,3,1,0:T(8,128)S(1)} fusion(f32[8,32,32,32]{3,2,1,0:T(8,128)} %reshape.220, f32[8,3,32,32]{2,3,0,1:T(8,128)S(1)} %broadcast_select_fusion), kind=kOutput, calls=%fused_computation.35 | convolution fusion | flops 100663296 | bytes 2228224 | tf_op jit(solution)/shard_map/isabc,icd->isabd/dot_general | solution.py:37
  39.2 9.3 %fusion.14 = f32[8,32,32,32]{1,2,3,0:T(8,128)} fusion(f32[8,32,32,32]{2,3,1,0:T(8,128)S(1)} %convolution_bitcast_fusion.3, f32[8,3,32,32]{2,3,0,1:T(8,128)S(1)} %broadcast_select_fusion), kind=kOutput, calls=%fused_computation.23 | convolution fusion | flops 100663296 | bytes 5373952 | tf_op jit(solution)/shard_map/isabd,iag->isgbd/dot_general | solution.py:40
  48.5 20.7 %convolution_bitcast_fusion.2 = f32[8,32,32,32]{3,2,1,0:T(8,128)} fusion(f32[8,32,32,32]{2,3,1,0:T(8,128)S(1)} %convolution_bitcast_fusion.3, f32[8,3,32,32]{2,3,0,1:T(8,128)S(1)} %broadcast_select_fusion), kind=kOutput, calls=%fused_computation.34 | convolution fusion | flops 100663296 | bytes 5373952 | tf_op jit(solution)/shard_map/isabd,ibe->isaed/dot_general | solution.py:38
  69.2 6.8 %fusion.20 = f32[8,32,32,32]{3,1,2,0:T(8,128)} fusion(f32[8,32,32,32]{3,2,1,0:T(8,128)S(1)} %copy-done.1, f32[8,3,32,32]{2,3,0,1:T(8,128)S(1)} %broadcast_select_fusion), kind=kOutput, calls=%fused_computation.29 | convolution fusion | flops 100663296 | bytes 5373952 | tf_op jit(solution)/shard_map/isabc,iag->isgbc/dot_general | solution.py:32
  76.1 6.8 %copy.93 = f32[8,32,32,32]{2,1,3,0:T(8,128)} copy(f32[8,32,32,32]{3,2,1,0:T(8,128)} %convolution_bitcast_fusion.2) | data formatting | bytes 2097152 | tf_op jit(solution)/shard_map/reshape.51
  82.9 9.7 %convolution_bitcast_fusion.7 = f32[8,1,32,32]{3,2,0,1:T(8,128)S(1)} fusion(f32[8,32,32,32]{1,2,3,0:T(8,128)} %fusion.14, f32[8,32,32,32]{2,1,3,0:T(8,128)} %copy.94), kind=kOutput, calls=%fused_computation.43 | convolution fusion | flops 100663296 | bytes 2129920 | tf_op jit(solution)/shard_map/isgbd,isghd->ibh/dot_general | solution.py:41
  92.7 4.1 convolution_bitcast_fusion.8
  96.8 6.3 %fusion.12 = f32[8,32,32,32]{3,1,2,0:T(8,128)S(1)} fusion(f32[8,32,32,32]{3,1,2,0:T(8,128)S(1)} %copy-done.8, f32[8,3,32,32]{2,3,0,1:T(8,128)S(1)} %broadcast_select_fusion), kind=kOutput, calls=%fused_computation.21 | convolution fusion | flops 100663296 | bytes 5373952 | tf_op jit(solution)/shard_map/isgbc,ibe->isgec/dot_general | solution.py:33
  103.2 7.0 %fusion.28 = f32[8,1,32,32]{3,2,0,1:T(8,128)S(1)} fusion(f32[8,32,32,32]{3,2,1,0:T(8,128)S(1)} %copy-done.2, f32[8,32,32,32]{3,1,2,0:T(8,128)S(1)} %fusion.12), kind=kOutput, calls=%fused_computation.39 | convolution fusion | flops 100663296 | bytes 2129920 | tf_op jit(solution)/shard_map/isgec,isgek->ick/dot_general | solution.py:43
  111.4 2.7 reshape.341
  115.2 17.2 %all-reduce.5.cloned.1.call-done = f32[8,3,32,32]{3,2,0,1:T(8,128)} async-done(((f32[8,3,32,32]{3,2,0,1:T(8,128)}), f32[8,3,32,32]{3,2,0,1:T(8,128)}) %all-reduce.5.cloned.1.call-update) | async-done | bytes 98320 | tf_op jit(solution)/shard_map/psum | solution.py:85
  135.4 49.6 %all-gather.2 = f32[16,10,1024]{2,1,0:T(8,128)} all-gather(f32[1,10,1024]{2,1,0:T(8,128)S(1)} %bitcast.196), channel_id=2, replica_groups=mesh['region'=16,'blk'=2] {'region'}, dimensions={0}, use_global_device_ids=true | all-gather | bytes 696320 | tf_op jit(solution)/shard_map/all_gather | solution.py:88
  187.8 21.4 %convolution_bitcast_fusion.1 = f32[8,32,32,32]{2,3,1,0:T(8,128)S(1)} fusion(f32[8,32,32,32]{3,2,1,0:T(8,128)} %reshape.220, f32[8,3,32,32]{3,2,1,0:T(8,128)S(1)} %reshape.224), kind=kOutput, calls=%fused_computation.33 | convolution fusion | flops 100663296 | bytes 2228224 | tf_op jit(solution)/shard_map/isabc,icd->isabd/dot_general | solution.py:37
  209.3 8.4 %fusion.10 = f32[8,32,32,32]{1,2,3,0:T(8,128)S(1)} fusion(f32[8,32,32,32]{2,3,1,0:T(8,128)S(1)} %convolution_bitcast_fusion.1, f32[8,3,32,32]{3,2,1,0:T(8,128)S(1)} %reshape.224), kind=kOutput, calls=%fused_computation.19 | convolution fusion | flops 100663296 | bytes 5373952 | tf_op jit(solution)/shard_map/isabd,iag->isgbd/dot_general | solution.py:40
  217.7 20.9 %convolution_bitcast_fusion = f32[8,32,32,32]{3,2,1,0:T(8,128)} fusion(f32[8,32,32,32]{2,3,1,0:T(8,128)S(1)} %convolution_bitcast_fusion.1, f32[8,3,32,32]{3,2,1,0:T(8,128)S(1)} %reshape.224), kind=kOutput, calls=%fused_computation.32 | convolution fusion | flops 100663296 | bytes 5373952 | tf_op jit(solution)/shard_map/isabd,ibe->isaed/dot_general | solution.py:38
  238.6 6.9 %fusion.18 = f32[8,32,32,32]{3,1,2,0:T(8,128)} fusion(f32[8,32,32,32]{3,2,1,0:T(8,128)S(1)} %copy-done.3, f32[8,3,32,32]{3,2,1,0:T(8,128)S(1)} %reshape.224), kind=kOutput, calls=%fused_computation.27 | convolution fusion | flops 100663296 | bytes 5373952 | tf_op jit(solution)/shard_map/isabc,iag->isgbc/dot_general | solution.py:32
  245.5 6.0 %convolution_bitcast_fusion.5 = f32[8,1,32,32]{3,2,0,1:T(8,128)S(1)} fusion(f32[8,32,32,32]{1,2,3,0:T(8,128)S(1)} %fusion.10, f32[8,32,32,32]{2,1,3,0:T(8,128)S(1)} %copy-done.6), kind=kOutput, calls=%fused_computation.41 | convolution fusion | flops 100663296 | bytes 2129920 | tf_op jit(solution)/shard_map/isgbd,isghd->ibh/dot_general | solution.py:41
  251.5 6.8 %copy.109 = f32[8,32,32,32]{2,1,3,0:T(8,128)} copy(f32[8,32,32,32]{3,2,1,0:T(8,128)} %convolution_bitcast_fusion) | data formatting | bytes 2097152 | tf_op jit(solution)/shard_map/reshape.70
  258.3 7.7 %convolution_bitcast_fusion.6 = f32[8,1,32,32]{3,2,0,1:T(8,128)S(1)} fusion(f32[8,32,32,32]{2,1,3,0:T(8,128)} %copy.109, f32[8,32,32,32]{2,1,3,0:T(8,128)} %copy.94), kind=kOutput, calls=%fused_computation.42 | convolution fusion | flops 100663296 | bytes 2129920 | tf_op jit(solution)/shard_map/isaed,isfed->iaf/dot_general | solution.py:39
  266.0 6.2 %fusion.8 = f32[8,32,32,32]{3,1,2,0:T(8,128)S(1)} fusion(f32[8,32,32,32]{3,1,2,0:T(8,128)S(1)} %copy-done.7, f32[8,3,32,32]{3,2,1,0:T(8,128)S(1)} %reshape.224), kind=kOutput, calls=%fused_computation.17 | convolution fusion | flops 100663296 | bytes 5373952 | tf_op jit(solution)/shard_map/isgbc,ibe->isgec/dot_general | solution.py:33
  272.2 7.1 %fusion.31 = f32[8,1,32,32]{3,2,0,1:T(8,128)S(1)} fusion(f32[8,32,32,32]{3,2,1,0:T(8,128)S(1)} %copy-done.4, f32[8,32,32,32]{3,1,2,0:T(8,128)S(1)} %fusion.8), kind=kOutput, calls=%fused_computation.40 | convolution fusion | flops 100663296 | bytes 2129920 | tf_op jit(solution)/shard_map/isgec,isgek->ick/dot_general | solution.py:43
  280.3 14.4 %all-reduce.7.cloned.1.call-done = f32[8,3,32,32]{3,2,0,1:T(8,128)} async-done(((f32[8,3,32,32]{3,2,0,1:T(8,128)}), f32[8,3,32,32]{3,2,0,1:T(8,128)}) %all-reduce.7.cloned.1.call-update) | async-done | bytes 98320 | tf_op jit(solution)/shard_map/psum | solution.py:85
  297.7 49.6 %all-gather.3 = f32[16,10,1024]{2,1,0:T(8,128)} all-gather(f32[1,10,1024]{2,1,0:T(8,128)S(1)} %bitcast.195), channel_id=3, replica_groups=mesh['region'=16,'blk'=2] {'region'}, dimensions={0}, use_global_device_ids=true | all-gather | bytes 696320 | tf_op jit(solution)/shard_map/all_gather | solution.py:88
  350.1 8.3 %fusion.16 = f32[8,32,32,32]{3,1,2,0:T(8,128)S(1)} fusion(f32[8,32,32,32]{3,2,1,0:T(8,128)} %reshape.220, f32[8,3,32,32]{3,2,1,0:T(8,128)S(1)} %reshape.228), kind=kOutput, calls=%fused_computation.25 | convolution fusion | flops 100663296 | bytes 2228224 | tf_op jit(solution)/shard_map/isabc,iag->isgbc/dot_general | solution.py:32
  358.5 5.6 %fusion.25 = bf16[8,32,32,32]{3,1,2,0:T(8,128)(2,1)S(1)} fusion(f32[8,32,32,32]{3,1,2,0:T(8,128)S(1)} %fusion.16, f32[8,3,32,32]{3,2,1,0:T(8,128)S(1)} %reshape.228), kind=kOutput, calls=%fused_computation.36 | convolution fusion | flops 100925440 | bytes 4849664 | tf_op jit(solution)/shard_map/isgbc,ibe->isgec/dot_general | solution.py:33
  365.3 1.9 all_gather.11
  368.2 5.6 %collective-permute-start.1 = (bf16[2,4096]{1,0:T(2,128)(2,1)S(1)}, bf16[2,4096]{1,0:T(2,128)(2,1)S(1)}, u32[]{:S(2)}, u32[]{:S(2)}) collective-permute-start(bf16[2,4096]{1,0:T(2,128)(2,1)S(1)} %gather_fusion.6), channel_id=1, source_target_pairs={{0,30},{2,0},{4,2},{6,4},{8,6},{10,8},{12,10},{14,12},{16,14},{18,... | collective-permute-start | bytes 49160 | tf_op jit(solution)/shard_map/ppermute | solution.py:24
  373.9 1.6 collective-permute-done
  375.6 5.6 %collective-permute-start.3 = (bf16[2,4096]{1,0:T(2,128)(2,1)S(1)}, bf16[2,4096]{1,0:T(2,128)(2,1)S(1)}, u32[]{:S(2)}, u32[]{:S(2)}) collective-permute-start(bf16[2,4096]{1,0:T(2,128)(2,1)S(1)} %collective-permute-done.1), channel_id=1, source_target_pairs={{0,30},{2,0},{4,2},{6,4},{8,6},{10,8},{12,10},{14,12},{16,14},{18,... | collective-permute-start | bytes 49160 | tf_op jit(solution)/shard_map/ppermute | solution.py:24
  381.2 1.6 collective-permute-done.2
  382.9 5.6 %collective-permute-start.5 = (bf16[2,4096]{1,0:T(2,128)(2,1)S(1)}, bf16[2,4096]{1,0:T(2,128)(2,1)S(1)}, u32[]{:S(2)}, u32[]{:S(2)}) collective-permute-start(bf16[2,4096]{1,0:T(2,128)(2,1)S(1)} %collective-permute-done.3), channel_id=1, source_target_pairs={{0,30},{2,0},{4,2},{6,4},{8,6},{10,8},{12,10},{14,12},{16,14},{18,... | collective-permute-start | bytes 49160 | tf_op jit(solution)/shard_map/ppermute | solution.py:24
  388.6 1.6 collective-permute-done.4
  390.2 5.6 %collective-permute-start.7 = (bf16[2,4096]{1,0:T(2,128)(2,1)S(1)}, bf16[2,4096]{1,0:T(2,128)(2,1)S(1)}, u32[]{:S(2)}, u32[]{:S(2)}) collective-permute-start(bf16[2,4096]{1,0:T(2,128)(2,1)S(1)} %collective-permute-done.5), channel_id=1, source_target_pairs={{0,30},{2,0},{4,2},{6,4},{8,6},{10,8},{12,10},{14,12},{16,14},{18,... | collective-permute-start | bytes 49160 | tf_op jit(solution)/shard_map/ppermute | solution.py:24
  395.9 1.6 collective-permute-done.6
  397.6 5.6 %collective-permute-start.9 = (bf16[2,4096]{1,0:T(2,128)(2,1)S(1)}, bf16[2,4096]{1,0:T(2,128)(2,1)S(1)}, u32[]{:S(2)}, u32[]{:S(2)}) collective-permute-start(bf16[2,4096]{1,0:T(2,128)(2,1)S(1)} %collective-permute-done.7), channel_id=1, source_target_pairs={{0,30},{2,0},{4,2},{6,4},{8,6},{10,8},{12,10},{14,12},{16,14},{18,... | collective-permute-start | bytes 49160 | tf_op jit(solution)/shard_map/ppermute | solution.py:24
  403.2 1.6 collective-permute-done.8
  404.9 5.6 %collective-permute-start.11 = (bf16[2,4096]{1,0:T(2,128)(2,1)S(1)}, bf16[2,4096]{1,0:T(2,128)(2,1)S(1)}, u32[]{:S(2)}, u32[]{:S(2)}) collective-permute-start(bf16[2,4096]{1,0:T(2,128)(2,1)S(1)} %collective-permute-done.9), channel_id=1, source_target_pairs={{0,30},{2,0},{4,2},{6,4},{8,6},{10,8},{12,10},{14,12},{16,14},{18,... | collective-permute-start | bytes 49160 | tf_op jit(solution)/shard_map/ppermute | solution.py:24
  412.2 5.6 %collective-permute-start.13 = (bf16[2,4096]{1,0:T(2,128)(2,1)S(1)}, bf16[2,4096]{1,0:T(2,128)(2,1)S(1)}, u32[]{:S(2)}, u32[]{:S(2)}) collective-permute-start(bf16[2,4096]{1,0:T(2,128)(2,1)S(1)} %collective-permute-done.11), channel_id=1, source_target_pairs={{0,30},{2,0},{4,2},{6,4},{8,6},{10,8},{12,10},{14,12},{16,14},{18,... | collective-permute-start | bytes 49160 | tf_op jit(solution)/shard_map/ppermute | solution.py:24
  419.6 7.3 %collective-permute-done.14 = bf16[2,4096]{1,0:T(2,128)(2,1)S(1)} collective-permute-done((bf16[2,4096]{1,0:T(2,128)(2,1)S(1)}, bf16[2,4096]{1,0:T(2,128)(2,1)S(1)}, u32[]{:S(2)}, u32[]{:S(2)}) %collective-permute-start.14) | collective-permute-done | bytes 16416 | tf_op jit(solution)/shard_map/ppermute | solution.py:21
  429.8 24.5 %fusion.22 = f32[8,2,32,32,32]{3,4,2,1,0:T(8,128)} fusion(f32[8,32,32,32,1]{3,2,1,0,4:T(8,128)} %reshape.341, f32[8,2,32,32,1]{3,1,2,0,4:T(2,128)S(1)} %bitcast.194), kind=kOutput, calls=%fused_computation.31 | convolution fusion | flops 201326592 | bytes 3211264 | tf_op jit(solution)/shard_map/iuvc,iacn->iauvn/dot_general | solution.py:114
  454.4 9.0 %copy.129 = f32[8,2,32,32,32]{4,3,2,1,0:T(8,128)} copy(f32[8,2,32,32,32]{3,4,2,1,0:T(8,128)} %fusion.22) | data formatting | bytes 4194304 | tf_op jit(solution)/shard_map/iuvc,iacn->iauvn/transpose | solution.py:114
  463.3 7.7 %reshape.233 = f32[8,2,32,1024]{3,2,1,0:T(8,128)} reshape(f32[8,2,32,32,32]{4,3,2,1,0:T(8,128)} %copy.129) | data formatting | bytes 4194304 | tf_op jit(solution)/shard_map/reshape | solution.py:115
  471.7 16.6 %all-reduce.9.cloned.1.call-done = f32[8,2,32,1024]{3,2,1,0:T(8,128)} async-done(((f32[8,2,32,1024]{3,2,1,0:T(8,128)}), f32[8,2,32,1024]{3,2,1,0:T(8,128)}) %all-reduce.9.cloned.1.call-update) | async-done | bytes 2097168
  488.3 2.0 multiply_reduce_fusion
  491.1 2.4 psum.23
  493.5 3.1 divide_select_fusion
  (150 shorter events, 25.4 us)
Async XLA Ops:
  7.2 357.0 %copy-start = (bf16[8,2,32,1024]{3,2,1,0:T(8,128)(2,1)S(1)}, bf16[8,2,32,1024]{3,2,1,0:T(8,128)(2,1)}, u32[]{:S(2)}) copy-start(bf16[8,2,32,1024]{3,2,1,0:T(8,128)(2,1)} %param.12) | copy-start | bytes 3145732
  7.2 125.2 %all-reduce.5.cloned.1.call-start = ((), (), s32[]{:S(2)}) async-start(), calls=%async_computation | async-start | bytes 786432 | tf_op jit(solution)/shard_map/psum | solution.py:85
  11.9 6.4 %copy-start.12 = (f32[32,32]{0,1:T(8,128)S(1)}, f32[32,32]{0,1:T(8,128)}, u32[]{:S(2)}) copy-start(f32[32,32]{0,1:T(8,128)} %constant.158.clone.1) | copy-start | bytes 12292
  48.5 20.7 %copy-start.1 = (f32[8,32,32,32]{3,2,1,0:T(8,128)S(1)}, f32[8,32,32,32]{3,2,1,0:T(8,128)}, u32[]{:S(2)}) copy-start(f32[8,32,32,32]{3,2,1,0:T(8,128)} %reshape.220) | copy-start | bytes 3145732
  82.9 9.8 %copy-start.5 = (f32[8,32,32,32]{2,1,3,0:T(8,128)S(1)}, f32[8,32,32,32]{2,1,3,0:T(8,128)}, u32[]{:S(2)}) copy-start(f32[8,32,32,32]{2,1,3,0:T(8,128)} %copy.94) | copy-start | bytes 3145732
  82.9 9.8 %copy-start.9 = (f32[8,32,32,32]{2,1,3,0:T(8,128)S(1)}, f32[8,32,32,32]{2,1,3,0:T(8,128)}, u32[]{:S(2)}) copy-start(f32[8,32,32,32]{2,1,3,0:T(8,128)} %copy.93) | copy-start | bytes 3145732
  92.7 4.1 copy-start.8
  96.8 6.3 %copy-start.2 = (f32[8,32,32,32]{3,2,1,0:T(8,128)S(1)}, f32[8,32,32,32]{3,2,1,0:T(8,128)}, u32[]{:S(2)}) copy-start(f32[8,32,32,32]{3,2,1,0:T(8,128)} %reshape.220) | copy-start | bytes 3145732
  103.1 8.2 %copy-start.13 = (s32[8,3]{0,1:T(4,128)S(1)}, s32[8,3]{0,1:T(4,128)}, u32[]{:S(2)}) copy-start(s32[8,3]{0,1:T(4,128)} %param.14) | copy-start | bytes 292
  103.2 8.2 %copy-start.10 = (f32[8,1,32,1024]{3,2,1,0:T(8,128)S(1)}, f32[8,1,32,1024]{3,2,1,0:T(8,128)}, u32[]{:S(2)}) copy-start(f32[8,1,32,1024]{3,2,1,0:T(8,128)} %param.11) | copy-start | bytes 3145732
  110.1 4.0 copy-start.16
  110.1 4.0 copy-start.17
  110.2 4.0 copy-start.18
  110.2 4.0 copy-start.19
  110.2 4.3 copy-start.15
  110.2 4.5 copy-start.14
  111.0 183.7 %all-reduce.7.cloned.1.call-start = ((), (), s32[]{:S(2)}) async-start(), calls=%async_computation.1 | async-start | bytes 786432 | tf_op jit(solution)/shard_map/psum | solution.py:85
  114.1 72.9 %copy-start.11 = (f32[1,1024]{1,0:T(1,128)S(1)}, f32[1,1024]{1,0:T(1,128)}, u32[]{:S(2)}) copy-start(f32[1,1024]{1,0:T(1,128)} %constant.167.clone.1) | copy-start | bytes 12292
  217.7 20.9 %copy-start.3 = (f32[8,32,32,32]{3,2,1,0:T(8,128)S(1)}, f32[8,32,32,32]{3,2,1,0:T(8,128)}, u32[]{:S(2)}) copy-start(f32[8,32,32,32]{3,2,1,0:T(8,128)} %reshape.220) | copy-start | bytes 3145732
  238.6 6.9 %copy-start.6 = (f32[8,32,32,32]{2,1,3,0:T(8,128)S(1)}, f32[8,32,32,32]{2,1,3,0:T(8,128)}, u32[]{:S(2)}) copy-start(f32[8,32,32,32]{2,1,3,0:T(8,128)} %copy.94) | copy-start | bytes 3145732
  258.3 7.7 %copy-start.7 = (f32[8,32,32,32]{3,1,2,0:T(8,128)S(1)}, f32[8,32,32,32]{3,1,2,0:T(8,128)}, u32[]{:S(2)}) copy-start(f32[8,32,32,32]{3,1,2,0:T(8,128)} %fusion.18) | copy-start | bytes 3145732
  266.0 6.2 %copy-start.4 = (f32[8,32,32,32]{3,2,1,0:T(8,128)S(1)}, f32[8,32,32,32]{3,2,1,0:T(8,128)}, u32[]{:S(2)}) copy-start(f32[8,32,32,32]{3,2,1,0:T(8,128)} %reshape.220) | copy-start | bytes 3145732
  280.2 208.1 %all-reduce.9.cloned.1.call-start = ((), (), s32[]{:S(2)}) async-start(), calls=%async_computation.2 | async-start | bytes 4194304
  367.9 7.6 %collective-permute-start = (bf16[2,4096]{1,0:T(2,128)(2,1)S(1)}, bf16[2,4096]{1,0:T(2,128)(2,1)S(1)}, u32[]{:S(2)}, u32[]{:S(2)}) collective-permute-start(bf16[2,4096]{1,0:T(2,128)(2,1)S(1)} %gather_fusion.6), channel_id=1, source_target_pairs={{0,2},{2,4},{4,6},{6,8},{8,10},{10,12},{12,14},{14,16},{16,18},{18... | collective-permute-start | bytes 49160 | tf_op jit(solution)/shard_map/ppermute | solution.py:21
  368.2 7.3 %collective-permute-start.1 = (bf16[2,4096]{1,0:T(2,128)(2,1)S(1)}, bf16[2,4096]{1,0:T(2,128)(2,1)S(1)}, u32[]{:S(2)}, u32[]{:S(2)}) collective-permute-start(bf16[2,4096]{1,0:T(2,128)(2,1)S(1)} %gather_fusion.6), channel_id=1, source_target_pairs={{0,30},{2,0},{4,2},{6,4},{8,6},{10,8},{12,10},{14,12},{16,14},{18,... | collective-permute-start | bytes 49160 | tf_op jit(solution)/shard_map/ppermute | solution.py:24
  375.5 7.3 %collective-permute-start.2 = (bf16[2,4096]{1,0:T(2,128)(2,1)S(1)}, bf16[2,4096]{1,0:T(2,128)(2,1)S(1)}, u32[]{:S(2)}, u32[]{:S(2)}) collective-permute-start(bf16[2,4096]{1,0:T(2,128)(2,1)S(1)} %collective-permute-done), channel_id=1, source_target_pairs={{0,2},{2,4},{4,6},{6,8},{8,10},{10,12},{12,14},{14,16},{16,18},{18... | collective-permute-start | bytes 49160 | tf_op jit(solution)/shard_map/ppermute | solution.py:21
  375.6 7.3 %collective-permute-start.3 = (bf16[2,4096]{1,0:T(2,128)(2,1)S(1)}, bf16[2,4096]{1,0:T(2,128)(2,1)S(1)}, u32[]{:S(2)}, u32[]{:S(2)}) collective-permute-start(bf16[2,4096]{1,0:T(2,128)(2,1)S(1)} %collective-permute-done.1), channel_id=1, source_target_pairs={{0,30},{2,0},{4,2},{6,4},{8,6},{10,8},{12,10},{14,12},{16,14},{18,... | collective-permute-start | bytes 49160 | tf_op jit(solution)/shard_map/ppermute | solution.py:24
  382.9 7.3 %collective-permute-start.4 = (bf16[2,4096]{1,0:T(2,128)(2,1)S(1)}, bf16[2,4096]{1,0:T(2,128)(2,1)S(1)}, u32[]{:S(2)}, u32[]{:S(2)}) collective-permute-start(bf16[2,4096]{1,0:T(2,128)(2,1)S(1)} %collective-permute-done.2), channel_id=1, source_target_pairs={{0,2},{2,4},{4,6},{6,8},{8,10},{10,12},{12,14},{14,16},{16,18},{18... | collective-permute-start | bytes 49160 | tf_op jit(solution)/shard_map/ppermute | solution.py:21
  382.9 7.3 %collective-permute-start.5 = (bf16[2,4096]{1,0:T(2,128)(2,1)S(1)}, bf16[2,4096]{1,0:T(2,128)(2,1)S(1)}, u32[]{:S(2)}, u32[]{:S(2)}) collective-permute-start(bf16[2,4096]{1,0:T(2,128)(2,1)S(1)} %collective-permute-done.3), channel_id=1, source_target_pairs={{0,30},{2,0},{4,2},{6,4},{8,6},{10,8},{12,10},{14,12},{16,14},{18,... | collective-permute-start | bytes 49160 | tf_op jit(solution)/shard_map/ppermute | solution.py:24
  390.2 7.3 %collective-permute-start.6 = (bf16[2,4096]{1,0:T(2,128)(2,1)S(1)}, bf16[2,4096]{1,0:T(2,128)(2,1)S(1)}, u32[]{:S(2)}, u32[]{:S(2)}) collective-permute-start(bf16[2,4096]{1,0:T(2,128)(2,1)S(1)} %collective-permute-done.4), channel_id=1, source_target_pairs={{0,2},{2,4},{4,6},{6,8},{8,10},{10,12},{12,14},{14,16},{16,18},{18... | collective-permute-start | bytes 49160 | tf_op jit(solution)/shard_map/ppermute | solution.py:21
  390.2 7.3 %collective-permute-start.7 = (bf16[2,4096]{1,0:T(2,128)(2,1)S(1)}, bf16[2,4096]{1,0:T(2,128)(2,1)S(1)}, u32[]{:S(2)}, u32[]{:S(2)}) collective-permute-start(bf16[2,4096]{1,0:T(2,128)(2,1)S(1)} %collective-permute-done.5), channel_id=1, source_target_pairs={{0,30},{2,0},{4,2},{6,4},{8,6},{10,8},{12,10},{14,12},{16,14},{18,... | collective-permute-start | bytes 49160 | tf_op jit(solution)/shard_map/ppermute | solution.py:24
  397.6 7.3 %collective-permute-start.8 = (bf16[2,4096]{1,0:T(2,128)(2,1)S(1)}, bf16[2,4096]{1,0:T(2,128)(2,1)S(1)}, u32[]{:S(2)}, u32[]{:S(2)}) collective-permute-start(bf16[2,4096]{1,0:T(2,128)(2,1)S(1)} %collective-permute-done.6), channel_id=1, source_target_pairs={{0,2},{2,4},{4,6},{6,8},{8,10},{10,12},{12,14},{14,16},{16,18},{18... | collective-permute-start | bytes 49160 | tf_op jit(solution)/shard_map/ppermute | solution.py:21
  397.6 7.3 %collective-permute-start.9 = (bf16[2,4096]{1,0:T(2,128)(2,1)S(1)}, bf16[2,4096]{1,0:T(2,128)(2,1)S(1)}, u32[]{:S(2)}, u32[]{:S(2)}) collective-permute-start(bf16[2,4096]{1,0:T(2,128)(2,1)S(1)} %collective-permute-done.7), channel_id=1, source_target_pairs={{0,30},{2,0},{4,2},{6,4},{8,6},{10,8},{12,10},{14,12},{16,14},{18,... | collective-permute-start | bytes 49160 | tf_op jit(solution)/shard_map/ppermute | solution.py:24
  404.9 7.3 %collective-permute-start.10 = (bf16[2,4096]{1,0:T(2,128)(2,1)S(1)}, bf16[2,4096]{1,0:T(2,128)(2,1)S(1)}, u32[]{:S(2)}, u32[]{:S(2)}) collective-permute-start(bf16[2,4096]{1,0:T(2,128)(2,1)S(1)} %collective-permute-done.8), channel_id=1, source_target_pairs={{0,2},{2,4},{4,6},{6,8},{8,10},{10,12},{12,14},{14,16},{16,18},{18... | collective-permute-start | bytes 49160 | tf_op jit(solution)/shard_map/ppermute | solution.py:21
  404.9 7.3 %collective-permute-start.11 = (bf16[2,4096]{1,0:T(2,128)(2,1)S(1)}, bf16[2,4096]{1,0:T(2,128)(2,1)S(1)}, u32[]{:S(2)}, u32[]{:S(2)}) collective-permute-start(bf16[2,4096]{1,0:T(2,128)(2,1)S(1)} %collective-permute-done.9), channel_id=1, source_target_pairs={{0,30},{2,0},{4,2},{6,4},{8,6},{10,8},{12,10},{14,12},{16,14},{18,... | collective-permute-start | bytes 49160 | tf_op jit(solution)/shard_map/ppermute | solution.py:24
  412.2 7.3 %collective-permute-start.12 = (bf16[2,4096]{1,0:T(2,128)(2,1)S(1)}, bf16[2,4096]{1,0:T(2,128)(2,1)S(1)}, u32[]{:S(2)}, u32[]{:S(2)}) collective-permute-start(bf16[2,4096]{1,0:T(2,128)(2,1)S(1)} %collective-permute-done.10), channel_id=1, source_target_pairs={{0,2},{2,4},{4,6},{6,8},{8,10},{10,12},{12,14},{14,16},{16,18},{18... | collective-permute-start | bytes 49160 | tf_op jit(solution)/shard_map/ppermute | solution.py:21
  412.2 7.4 %collective-permute-start.13 = (bf16[2,4096]{1,0:T(2,128)(2,1)S(1)}, bf16[2,4096]{1,0:T(2,128)(2,1)S(1)}, u32[]{:S(2)}, u32[]{:S(2)}) collective-permute-start(bf16[2,4096]{1,0:T(2,128)(2,1)S(1)} %collective-permute-done.11), channel_id=1, source_target_pairs={{0,30},{2,0},{4,2},{6,4},{8,6},{10,8},{12,10},{14,12},{16,14},{18,... | collective-permute-start | bytes 49160 | tf_op jit(solution)/shard_map/ppermute | solution.py:24
  419.6 7.3 %collective-permute-start.14 = (bf16[2,4096]{1,0:T(2,128)(2,1)S(1)}, bf16[2,4096]{1,0:T(2,128)(2,1)S(1)}, u32[]{:S(2)}, u32[]{:S(2)}) collective-permute-start(bf16[2,4096]{1,0:T(2,128)(2,1)S(1)} %collective-permute-done.12), channel_id=1, source_target_pairs={{0,2},{2,4},{4,6},{6,8},{8,10},{10,12},{12,14},{14,16},{16,18},{18... | collective-permute-start | bytes 49160 | tf_op jit(solution)/shard_map/ppermute | solution.py:21
  463.3 7.8 %copy-start.20 = (u32[32]{0:T(128)S(1)}, u32[32]{0:T(128)}, u32[]{:S(2)}) copy-start(u32[32]{0:T(128)} %constant.199) | copy-start | bytes 388
Sparse Core Ops, SparseCore 0:
  111.1 21.1 all-reduce.4
  280.3 14.3 all-reduce.6
  471.2 17.0 all-reduce.8
